TPU v7x, 256 devices: a whole 4x4x8 slice. The times are simulated.
256 devices in a mesh: row: 32 (over z, y), col: 8 (over x, core).
Axes of the slice: x: 4, y: 4, z: 8, core: 2. Of those that a mesh axis runs over, the one named last changes fastest.
Arguments:
- leaf_inverse: bfloat16 [256, 1024, 1024], P(('row', 'col')), as said below
- leaf_rhs: bfloat16 [256, 1024, 512], P(('row', 'col')), may hold values from -6 to 6
- leaf_tiles: bfloat16 [256, 1024, 1024], P(('row', 'col')), may hold values from -0.046875 to 0.046875
- mid_inverse_t: bfloat16 [16, 1024, 1024], P('col', None, 'row'), as said below
- mid_rhs: bfloat16 [16, 1024, 512], P('col', 'row'), may hold values from -6 to 6
- mid_tiles: bfloat16 [16, 1024, 1024], P('col', None, 'row'), may hold values from -0.125 to 0.125
- top_inverse_t: bfloat16 [2, 1024, 1024], P(None, None, 'col'), as said below
- top_rhs: bfloat16 [2, 1024, 512], P(None, 'col'), may hold values from -6 to 6
- tile_lists: int32 [256, 1], P(('row', 'col')), may hold values from 0 to 1
Outputs:
- leaf_solved: bfloat16 [256, 1024, 512], P(('row', 'col'))
- mid_solved: bfloat16 [16, 1024, 512], P('col', 'row')
- top_solved: bfloat16 [2, 1024, 512], P(None, 'col')
Inputs may be any that keep to these rules, and one draw needn't show every extreme that they name: Each leaf_inverse[d] is zero above its diagonal and has diagonal entries between 0.75 and 1.25. Each mid_inverse_t[q] is zero below its diagonal and has diagonal entries between 0.75 and 1.25. Each top_inverse_t[b] is zero below its diagonal and has diagonal entries between 0.75 and 1.25.
All inputs are finite; a program needn't handle non-finite values.
Results may differ from a plain program's by a relative error of at most 0.0065.
Values may be sent and summed in bfloat16 or wider, within the bound.
A program may use at most 64 MiB of HBM per device.

v0:
```python
import jax
import jax.numpy as jnp
from jax import lax
from jax.sharding import PartitionSpec as P

NB = 2


def solve_piece(inverse_cols, piece):
    return lax.dot_general(
        inverse_cols, piece, (((1,), (1,)), ((0,), (0,))), preferred_element_type=jnp.float32
    )


def local(
    leaf_inverse,
    leaf_rhs,
    leaf_tiles,
    mid_inverse_t,
    mid_rhs,
    mid_tiles,
    top_inverse_t,
    top_rhs,
    tile_lists,
):
    slot_ids = jnp.arange(NB, dtype=jnp.int32)[:, None, None]
    solved_leaf = jnp.dot(leaf_inverse[0], leaf_rhs[0], preferred_element_type=jnp.float32).astype(
        jnp.bfloat16
    )
    leaf_update = jnp.dot(leaf_tiles[0], solved_leaf, preferred_element_type=jnp.float32)
    mid_terms = jnp.where(slot_ids == tile_lists[0, 0], leaf_update[None], 0.0)
    mid_share = lax.psum_scatter(mid_terms, "row", scatter_dimension=1, tiled=True)
    mid_resid = (mid_rhs.astype(jnp.float32) - mid_share).astype(jnp.bfloat16)
    mid_own = solve_piece(
        mid_inverse_t, lax.all_gather(mid_resid, "row", axis=1, tiled=True)
    ).astype(jnp.bfloat16)
    top_terms = lax.dot_general(
        mid_tiles, mid_own, (((2,), (1,)), ((0,), (0,))), preferred_element_type=jnp.float32
    )
    summed_rows = lax.psum(top_terms, "row")
    top_share = lax.psum_scatter(summed_rows, "col", scatter_dimension=1, tiled=True)
    top_resid = (top_rhs.astype(jnp.float32) - top_share).astype(jnp.bfloat16)
    top_own = solve_piece(
        top_inverse_t, lax.all_gather(top_resid, "col", axis=1, tiled=True)
    ).astype(jnp.bfloat16)
    return (solved_leaf[None], mid_own, top_own)


def solution(mesh):
    placed = (
        P(("row", "col"), None, None),
        P(("row", "col"), None, None),
        P(("row", "col"), None, None),
        P("col", None, "row"),
        P("col", "row", None),
        P("col", None, "row"),
        P(None, None, "col"),
        P(None, "col", None),
        P(("row", "col"), None),
    )
    return jax.shard_map(
        local,
        mesh=mesh,
        in_specs=placed,
        out_specs=(P(("row", "col"), None, None), P("col", "row", None), P(None, "col", None)),
        check_vma=False,
    )
```

profile of v0, /device:TPU:1, one launch (start us, length us, event | category | flops | bytes accessed | tf_op | source)
XLA Modules:
  0.0 552.6 jit_solution(14263055349112722870)
XLA Ops:
  7.2 0.0 reduce-scatter.3.cloned.1.call-start
  8.0 0.8 copy-done
  8.8 2.6 fusion.7
  11.4 1.0 copy-done.8
  12.4 1.2 fusion.4
  13.6 2.6 broadcast_select_fusion
  16.2 0.0 reduce-scatter.3.cloned.1.call-update
  16.2 0.0 all-gather.3.cloned.1.call-start
  16.3 219.7 %reduce-scatter.3.cloned.1.call-done = f32[2,32,512]{2,1,0:T(8,128)} async-done(((f32[2,1024,512]{2,1,0:T(8,128)}), f32[2,32,512]{2,1,0:T(8,128)}) %reduce-scatter.3.cloned.1.call-update) | async-done | bytes 131088 | tf_op jit(solution)/shard_map/reduce_scatter | solution.py:32
  235.9 1.5 subtract_convert_fusion.1
  237.5 0.0 reduce-scatter.5.cloned.1.call-start
  237.5 79.3 %all-gather.3.cloned.1.call-done = bf16[2,1024,512]{2,1,0:T(8,128)(2,1)} async-done(((bf16[2,32,512]{2,1,0:T(8,128)(2,1)}), bf16[2,1024,512]{2,1,0:T(8,128)(2,1)}) %all-gather.3.cloned.1.call-update) | async-done | bytes 2097168 | tf_op jit(solution)/shard_map/all_gather | solution.py:35
  316.8 2.0 convolution_convert_fusion.1
  318.9 2.7 convolution_bitcast_fusion
  321.6 0.0 reduce-scatter.5.cloned.1.call-update
  321.6 0.0 all-reduce.2.cloned.1.call-start
  321.7 38.7 %reduce-scatter.5.cloned.1.call-done = f32[2,128,512]{1,2,0:T(8,128)} async-done(((f32[2,1024,512]{1,2,0:T(8,128)}), f32[2,128,512]{1,2,0:T(8,128)}) %reduce-scatter.5.cloned.1.call-update) | async-done | bytes 524304 | tf_op jit(solution)/shard_map/reduce_scatter | solution.py:41
  360.4 0.0 all-gather.5.cloned.1.call-start
  360.4 0.2 copy.12
  360.6 148.4 %all-reduce.2.cloned.1.call-done = f32[2,128,512]{1,2,0:T(8,128)} async-done(((f32[2,128,512]{1,2,0:T(8,128)}), f32[2,128,512]{1,2,0:T(8,128)}) %all-reduce.2.cloned.1.call-update) | async-done | bytes 524304 | tf_op jit(solution)/shard_map/psum | solution.py:40
  509.0 1.8 subtract_convert_fusion
  510.8 32.1 %all-gather.5.cloned.1.call-done = bf16[2,1024,512]{1,2,0:T(8,128)(2,1)} async-done(((bf16[2,128,512]{1,2,0:T(8,128)(2,1)}), bf16[2,1024,512]{1,2,0:T(8,128)(2,1)}) %all-gather.5.cloned.1.call-update) | async-done | bytes 2097168 | tf_op jit(solution)/shard_map/all_gather | solution.py:44
  542.9 2.3 fusion.10
  545.2 0.9 copy.13
  (20 shorter events, 0.1 us)
Async XLA Ops:
  7.2 1.6 copy-start
  7.2 228.7 %reduce-scatter.3.cloned.1.call-start = ((), (), s32[]{:S(2)}) async-start(), calls=%async_computation.2 | async-start | bytes 4325376 | tf_op jit(solution)/shard_map/reduce_scatter | solution.py:32
  8.8 3.6 copy-start.6
  11.4 1.0 copy-start.8
  16.2 219.7 %copy-start.5 = (bf16[2,32,512]{2,1,0:T(8,128)(2,1)S(1)}, bf16[2,32,512]{2,1,0:T(8,128)(2,1)}, u32[]{:S(2)}) copy-start(bf16[2,32,512]{2,1,0:T(8,128)(2,1)} %param.13) | copy-start | bytes 196612
  16.2 300.6 %copy-start.3 = (bf16[2,1024,32]{1,2,0:T(8,128)(2,1)S(1)}, bf16[2,1024,32]{1,2,0:T(8,128)(2,1)}, u32[]{:S(2)}) copy-start(bf16[2,1024,32]{1,2,0:T(8,128)(2,1)} %param.12) | copy-start | bytes 393220
  16.2 302.6 %copy-start.4 = (bf16[2,1024,32]{1,2,0:T(8,128)(2,1)S(1)}, bf16[2,1024,32]{1,2,0:T(8,128)(2,1)}, u32[]{:S(2)}) copy-start(bf16[2,1024,32]{1,2,0:T(8,128)(2,1)} %param.14) | copy-start | bytes 393220
  16.2 300.6 %all-gather.3.cloned.1.call-start = ((), (), s32[]{:S(2)}) async-start(), calls=%async_computation.3 | async-start | bytes 2162688 | tf_op jit(solution)/shard_map/all_gather | solution.py:35
  237.5 122.8 %reduce-scatter.5.cloned.1.call-start = ((), (), s32[]{:S(2)}) async-start(), calls=%async_computation.5 | async-start | bytes 4718592 | tf_op jit(solution)/shard_map/reduce_scatter | solution.py:41
  318.9 2.7 copy-start.1
  321.6 38.8 %copy-start.2 = (bf16[2,128,512]{2,1,0:T(8,128)(2,1)S(1)}, bf16[2,128,512]{2,1,0:T(8,128)(2,1)}, u32[]{:S(2)}) copy-start(bf16[2,128,512]{2,1,0:T(8,128)(2,1)} %param.16) | copy-start | bytes 786436
  321.6 221.3 %copy-start.7 = (bf16[2,1024,128]{2,1,0:T(8,128)(2,1)S(1)}, bf16[2,1024,128]{2,1,0:T(8,128)(2,1)}, u32[]{:S(2)}) copy-start(bf16[2,1024,128]{2,1,0:T(8,128)(2,1)} %param.15) | copy-start | bytes 1572868
  321.6 187.4 %all-reduce.2.cloned.1.call-start = ((), (), s32[]{:S(2)}) async-start(), calls=%async_computation.6 | async-start | bytes 1048576 | tf_op jit(solution)/shard_map/psum | solution.py:40
  360.4 182.6 %all-gather.5.cloned.1.call-start = ((), (), s32[]{:S(2)}) async-start(), calls=%async_computation.4 | async-start | bytes 2359296 | tf_op jit(solution)/shard_map/all_gather | solution.py:44
Sparse Core Ops, SparseCore 0:
  16.3 219.5 reduce-scatter.2
  239.4 77.3 all-gather.2
  321.7 38.5 reduce-scatter.4
  364.0 144.9 all-reduce.1
  511.2 31.6 all-gather.4
where the time goes:
time: 553 us
  waiting for transfers between devices  518 us (94%)
  between operations  14.7 us (3%)
  matrix products  10.9 us (2%)
  other arithmetic  5.91 us (1%)
    reduce_scatter x1, waiting for transfers between devices, local(): lax.psum_scatter(mid_terms, 'row', scatter_dimension=1, tiled=True)  220 us
    psum x1, waiting for transfers between devices, local(): summed_rows = lax.psum(top_terms, 'row')  148 us
    all_gather x1, waiting for transfers between devices, local(): lax.all_gather(mid_resid, 'row', axis=1, tiled=True)  79.3 us
    reduce_scatter x1, waiting for transfers between devices, local(): lax.psum_scatter(summed_rows, 'col', scatter_dimension=1, tiled=True)  38.7 us
    all_gather x1, waiting for transfers between devices, local(): lax.all_gather(top_resid, 'col', axis=1, tiled=True)  32.1 us
  transfers between devices with their start and end apart: 5, of which 5 were waited for; matrix products, arithmetic and copies ran while one was open for 0% of the time, Pallas kernels for 0%

commit v1 on v0

v1 whole, which is shorter than its diff:
```python
import functools
import jax
import jax.numpy as jnp
from jax import lax
from jax.experimental import pallas as pl
from jax.experimental.pallas import tpu as pltpu
from jax.sharding import PartitionSpec as P

MESH = pl.DeviceIdType.MESH
NZ, NY, NX, NK = 8, 4, 4, 2
NC = NX * NK
W = 1024
SRC = 512
CH = W // NZ
CS = SRC // NY
RB = 256
LAG = 4
F32 = jnp.float32
BF16 = jnp.bfloat16


def kernel(
    li, rhs, tiles, mi, mr, mt, ti, tr, tl,
    leaf_o, mid_o, top_o,
    liv, rv, tv, xv, usend, yrecv, ssend, srecv, rbuf,
    mig, mtg, mrv, flag, flagr, tiv, trv, ybf,
    pbuf, p32, crecv, qbuf, xrecv, zall, tall, tsend,
    load_sem, own_sem, y_s, y_r, mi_s, mi_r, mt_s, mt_r, mr_s, mr_r, fl_s, fl_r,
    s_s, s_r, r_s, r_r, c_s, c_r, x_s, x_r, z_s, z_r, t_s, t_r, mo_s, mo_r, to_s, to_r,
):
    row = lax.axis_index("row")
    col = lax.axis_index("col")
    z, y = row // NY, row % NY
    x, k = col // NK, col % NK

    def at_y(other):
        return (z * NY + other, col)

    def at_z(other):
        return (other * NY + y, col)

    def at_c(other):
        return (row, other)

    def remote(src, dst, s, r, device):
        return pltpu.make_async_remote_copy(
            src_ref=src, dst_ref=dst, send_sem=s, recv_sem=r, device_id=device, device_id_type=MESH
        )

    y_peers = [(y + d) % NY for d in range(1, NY)]

    rbuf[...] = jnp.zeros_like(rbuf)
    barrier = pltpu.get_barrier_semaphore()
    for other in y_peers:
        pl.semaphore_signal(barrier, inc=1, device_id=at_y(other), device_id_type=MESH)
    for d in range(1, NZ):
        pl.semaphore_signal(barrier, inc=1, device_id=at_z((z + d) % NZ), device_id_type=MESH)
    for d in range(1, NC):
        pl.semaphore_signal(barrier, inc=1, device_id=at_c((col + d) % NC), device_id_type=MESH)

    loads = {}

    def load(name, src, dst):
        copy = pltpu.make_async_copy(src, dst, load_sem.at[len(loads)])
        copy.start()
        loads[name] = copy

    for i in range(W // RB):
        rows = slice(i * RB, (i + 1) * RB)
        load(f"r{i}", rhs.at[0, rows, :], rv.at[rows, :])
        load(f"l{i}", li.at[0, rows, : (i + 1) * RB], liv.at[rows, : (i + 1) * RB])
    for i in range(W // RB):
        rows = slice(i * RB, (i + 1) * RB)
        load(f"t{i}", tiles.at[0, rows, :], tv.at[rows, :])
    own_cols = pl.ds(pl.multiple_of(y * CS, CS), CS)
    own_rows = pl.ds(pl.multiple_of(y * 32, 32), 32)
    load("mi", mi, mig.at[y])
    load("mr", mr.at[:, :, own_cols], mrv.at[:, own_rows, :])
    load("mt", mt, mtg.at[y])
    load("ti", ti, tiv)
    load("tr", tr.at[:, :, own_cols], trv)

    flag[...] = jnp.full(flag.shape, tl[0, 0].astype(F32))

    for i in range(W // RB):
        rows = slice(i * RB, (i + 1) * RB)
        loads[f"r{i}"].wait()
        loads[f"l{i}"].wait()
        xv[rows, :] = jnp.dot(
            liv[rows, : (i + 1) * RB], rv[: (i + 1) * RB, :], preferred_element_type=F32
        ).astype(BF16)
    leaf_copy = pltpu.make_async_copy(xv, leaf_o.at[0], own_sem.at[0])
    leaf_copy.start()

    pl.semaphore_wait(barrier, NY + NZ + NC - 3)

    sends = []

    def start(copy):
        copy.start()
        sends.append(copy)
        return copy

    fl_copies, mr_copies = [], []
    for n, other in enumerate(y_peers):
        fl_copies.append(start(remote(flag, flagr.at[n], fl_s.at[n], fl_r.at[n], at_y(other))))
        cols = pl.ds(pl.multiple_of(other * CS, CS), CS)
        mr_copies.append(
            start(remote(mr.at[:, :, cols], mrv.at[:, own_rows, :], mr_s.at[n], mr_r.at[n], at_y(other)))
        )

    def u_copy(j, n):
        return remote(
            usend.at[j, y_peers[n]], yrecv.at[n, j], y_s.at[n, j], y_r.at[n, j], at_y(y_peers[n])
        )

    for i in range(W // RB):
        rows = slice(i * RB, (i + 1) * RB)
        loads[f"t{i}"].wait()
        update = jnp.dot(tv[rows, :], xv[...], preferred_element_type=F32).astype(BF16)
        for h in range(RB // CH):
            j = i * (RB // CH) + h
            for s in range(NY):
                usend[j, s] = update[h * CH : (h + 1) * CH, s * CS : (s + 1) * CS]
            for n in (1, 0, 2):
                start(u_copy(j, n))

    def mi_copy(n):
        return remote(mi, mig.at[y], mi_s.at[n], mi_r.at[n], at_y(y_peers[n]))

    def mt_copy(n):
        return remote(mt, mtg.at[y], mt_s.at[n], mt_r.at[n], at_y(y_peers[n]))

    def s_copy(j):
        return remote(ssend.at[j], srecv.at[z], s_s.at[j], s_r.at[z], at_z(j))

    def r_copy(other):
        part = rbuf.at[:, pl.ds(pl.multiple_of(z * CH, CH), CH), :]
        return remote(part, part, r_s.at[other], r_r.at[z], at_z(other))

    for copy in fl_copies:
        copy.wait_recv()
    loads["mr"].wait()
    for copy in mr_copies:
        copy.wait_recv()

    def chunk(j):
        parts = [(usend[j, y].astype(F32), flag[0:1, :] > 0.5)]
        for n in range(NY - 1):
            u_copy(j, n).wait_recv()
            parts.append((yrecv[n, j].astype(F32), flagr[n, 0:1, :] > 0.5))
        one = sum(jnp.where(f, u, 0.0) for u, f in parts)
        zero = sum(jnp.where(f, 0.0, u) for u, f in parts)
        ssend[j, 0] = zero.astype(BF16)
        ssend[j, 1] = one.astype(BF16)

        @pl.when(z != j)
        def _():
            s_copy(j).start()

    def reduce_own():
        total = ssend[z].astype(F32)
        for d in range(1, NZ):
            other = (z + d) % NZ
            remote(ssend.at[0], srecv.at[other], s_s.at[0], s_r.at[other], at_z(other)).wait_recv()
            total += srecv[other].astype(F32)
        rbuf[:, pl.ds(pl.multiple_of(z * CH, CH), CH), :] = (mrv[...].astype(F32) - total).astype(BF16)
        for other in range(1, NZ):

            @pl.when(other > z)
            def _():
                r_copy(other).start()

    def step(j, carry):
        @pl.when(j < NZ)
        def _():
            chunk(j)

        @pl.when(j == 2)
        def _():
            for n in range(NY - 1):
                mi_copy(n).start()

        @pl.when(j == 5)
        def _():
            for n in range(NY - 1):
                mt_copy(n).start()

        @pl.when(z == j - LAG)
        def _():
            reduce_own()

        return carry

    lax.fori_loop(0, NZ + LAG, step, 0)

    loads["mi"].wait()
    for n in range(NY - 1):
        mi_copy(n).wait_recv()
    for other in range(NZ - 1):

        @pl.when(other < z)
        def _():
            part = rbuf.at[:, other * CH : (other + 1) * CH, :]
            remote(part, part, r_s.at[other], r_r.at[other], at_z(other)).wait_recv()

    turned = []
    for b in range(2):
        solved = jnp.dot(mig[:, b].reshape(CH, W), rbuf[b], preferred_element_type=F32)
        ybf[b] = solved.astype(BF16)
        turned.append(solved.T.astype(BF16))

    loads["mt"].wait()
    for n in range(NY - 1):
        mt_copy(n).wait_recv()
    for b in range(2):
        update = jnp.dot(turned[b], mtg[:, b].reshape(CH, W), preferred_element_type=F32)
        for c in range(NC):
            piece = update[:, c * CH : (c + 1) * CH]
            pbuf[c % NK, c // NK, b] = piece.astype(BF16)
            p32[c % NK, c // NK, b] = piece
    core_copy = start(
        remote(pbuf.at[1 - k], crecv, c_s.at[0], c_r.at[0], at_c(x * NK + 1 - k))
    )

    mid_copies = []
    for n, other in enumerate(y_peers):
        rows = pl.ds(pl.multiple_of(other * 32, 32), 32)
        mid_copies.append(
            start(remote(ybf.at[:, rows, :], mid_o.at[:, :, own_cols], mo_s.at[n], mo_r.at[n], at_y(other)))
        )
    mid_copy = pltpu.make_async_copy(ybf.at[:, own_rows, :], mid_o.at[:, :, own_cols], own_sem.at[1])
    mid_copy.start()

    loads["tr"].wait()
    rhs_t = [trv[b].astype(F32).T for b in range(2)]

    core_copy.wait_recv()
    x_copies = []
    for n in range(NX - 1):
        other = (x + n + 1) % NX
        qbuf[n] = (p32[k, other] + crecv[other].astype(F32)).astype(BF16)
        x_copies.append(
            start(remote(qbuf.at[n], xrecv.at[n], x_s.at[n], x_r.at[n], at_c(other * NK + k)))
        )
    total = p32[k, x] + crecv[x].astype(F32)
    for n in range(NX - 1):
        x_copies[n].wait_recv()
        total += xrecv[n].astype(F32)
    zall[z] = total.astype(BF16)
    for d in range(1, NZ):
        other = (z + d) % NZ
        start(remote(zall.at[z], zall.at[z], z_s.at[d - 1], z_r.at[z], at_z(other)))
    for d in range(1, NZ):
        other = (z + d) % NZ
        remote(zall.at[other], zall.at[other], z_s.at[d - 1], z_r.at[other], at_z(other)).wait_recv()

    mine = pl.ds(pl.multiple_of(col * CH, CH), CH)
    for b in range(2):
        total = zall[0, b].astype(F32)
        for d in range(1, NZ):
            total += zall[d, b].astype(F32)
        tall[b, :, mine] = (rhs_t[b] - total).astype(BF16)
    for d in range(1, NC):
        other = (col + d) % NC
        part = tall.at[:, :, mine]
        start(remote(part, part, t_s.at[d - 1], t_r.at[col], at_c(other)))
    loads["ti"].wait()
    for d in range(1, NC):
        other = (col + d) % NC
        part = tall.at[:, :, pl.ds(pl.multiple_of(other * CH, CH), CH)]
        remote(part, part, t_s.at[d - 1], t_r.at[other], at_c(other)).wait_recv()

    for b in range(2):
        solved = jnp.dot(tall[b], tiv[b], preferred_element_type=F32)
        tsend[b] = solved.T.astype(BF16)
    top_copies = []
    for n, other in enumerate(y_peers):
        top_copies.append(
            start(remote(tsend, top_o.at[:, :, own_cols], to_s.at[n], to_r.at[n], at_y(other)))
        )
    top_copy = pltpu.make_async_copy(tsend, top_o.at[:, :, own_cols], own_sem.at[2])
    top_copy.start()

    leaf_copy.wait()
    mid_copy.wait()
    for n in range(NY - 1):
        mi_copy(n).wait_send()
        mt_copy(n).wait_send()
        mid_copies[n].wait_recv()
    for j in range(NZ):

        @pl.when(z != j)
        def _():
            s_copy(j).wait_send()

        @pl.when(j > z)
        def _():
            r_copy(j).wait_send()

    for copy in sends:
        copy.wait_send()
    top_copy.wait()
    for copy in top_copies:
        copy.wait_recv()


def local(li, rhs, tiles, mi, mr, mt, ti, tr, tl):
    dma = pltpu.SemaphoreType.DMA
    vmem = pltpu.VMEM
    any_spec = pl.BlockSpec(memory_space=pl.ANY)
    n = NY - 1
    return pl.pallas_call(
        kernel,
        out_shape=(
            jax.ShapeDtypeStruct((1, W, SRC), BF16),
            jax.ShapeDtypeStruct((2, 32, SRC), BF16),
            jax.ShapeDtypeStruct((2, CH, SRC), BF16),
        ),
        in_specs=[pl.BlockSpec(memory_space=pltpu.HBM)] * 8 + [pl.BlockSpec(memory_space=pltpu.SMEM)],
        out_specs=(any_spec,) * 3,
        scratch_shapes=[
            vmem((W, W), BF16),
            vmem((W, SRC), BF16),
            vmem((W, W), BF16),
            vmem((W, SRC), BF16),
            vmem((NZ, NY, CH, CS), BF16),
            vmem((n, NZ, CH, CS), BF16),
            vmem((NZ, 2, CH, CS), BF16),
            vmem((NZ, 2, CH, CS), BF16),
            vmem((2, W, CS), BF16),
            vmem((NY, 2, 32, W), BF16),
            vmem((NY, 2, 32, W), BF16),
            vmem((2, CH, CS), BF16),
            vmem((8, 128), F32),
            vmem((n, 8, 128), F32),
            vmem((2, W, CH), BF16),
            vmem((2, CH, CS), BF16),
            vmem((2, CH, CS), BF16),
            vmem((NK, NX, 2, CS, CH), BF16),
            vmem((NK, NX, 2, CS, CH), F32),
            vmem((NX, 2, CS, CH), BF16),
            vmem((NX - 1, 2, CS, CH), BF16),
            vmem((NX - 1, 2, CS, CH), BF16),
            vmem((NZ, 2, CS, CH), BF16),
            vmem((2, CS, W), BF16),
            vmem((2, CH, CS), BF16),
            dma((17,)), dma((3,)),
            dma((n, NZ)), dma((n, NZ)),
            dma((n,)), dma((n,)), dma((n,)), dma((n,)),
            dma((n,)), dma((n,)), dma((n,)), dma((n,)),
            dma((NZ,)), dma((NZ,)), dma((NZ,)), dma((NZ,)),
            dma((1,)), dma((1,)), dma((NX - 1,)), dma((NX - 1,)),
            dma((NZ - 1,)), dma((NZ,)), dma((NC - 1,)), dma((NC,)),
            dma((n,)), dma((n,)), dma((n,)), dma((n,)),
        ],
        compiler_params=pltpu.CompilerParams(
            collective_id=0, has_side_effects=True, vmem_limit_bytes=56 * 1024 * 1024
        ),
        cost_estimate=pl.CostEstimate(flops=2_700_000_000, bytes_accessed=8_000_000, transcendentals=0),
        name="forward_substitution",
    )(li, rhs, tiles, jnp.swapaxes(mi, 1, 2), mr, jnp.swapaxes(mt, 1, 2), ti, tr, tl)


def solution(mesh):
    placed = (
        P(("row", "col"), None, None),
        P(("row", "col"), None, None),
        P(("row", "col"), None, None),
        P("col", None, "row"),
        P("col", "row", None),
        P("col", None, "row"),
        P(None, None, "col"),
        P(None, "col", None),
        P(("row", "col"), None),
    )
    return jax.shard_map(
        local,
        mesh=mesh,
        in_specs=placed,
        out_specs=(P(("row", "col"), None, None), P("col", "row", None), P(None, "col", None)),
        check_vma=False,
    )
```

time: 553 us -> 99.2 us (0.18)
  waiting for transfers between devices: 518 us -> 0 us
  Pallas kernels: 0 us -> 92.9 us
  between operations: 14.7 us -> 1.31 us
  matrix products: 10.9 us -> 0 us
  other arithmetic: 5.91 us -> 0 us
    reduce_scatter x2 -> x0, waiting for transfers between devices: 258 us -> none  [the longest x1 220 us: local(): lax.psum_scatter(mid_terms, 'row', scatter_dimension=1, tiled=True)]
    psum x1 -> x0, waiting for transfers between devices: 148 us -> none  [local(): summed_rows = lax.psum(top_terms, 'row')]
    all_gather x2 -> x0, waiting for transfers between devices: 111 us -> none  [the longest x1 79.3 us: local(): lax.all_gather(mid_resid, 'row', axis=1, tiled=True)]
    pallas_call x0 -> x1, Pallas kernels: none -> 92.9 us  [local(): pl.pallas_call(kernel, out_shape=(jax.ShapeDtypeStruct((1, W, SRC), BF16)...]
    dot_general x5 -> x0, matrix products: 10.9 us -> none  [the longest x2 4.32 us: solve_piece(): lax.dot_general(inverse_cols, piece, (((1,), (1,)), ((0,), (0,))), prefer...]
  transfers between devices with their start and end apart: 5 -> 0, of which waited for: 5 -> 0; matrix products, arithmetic and copies ran while one was open for 0% -> 0% of each run, Pallas kernels for 0% -> 0%
where the time goes in v1:
time: 99.2 us; the launch traced here: 97.9 us
  Pallas kernels  92.9 us (94%)
  local copies, waits for them, and re-layouts  3.65 us (4%)
  between operations  1.31 us (1%)
    pallas_call x1, Pallas kernels, local(): pl.pallas_call(kernel, out_shape=(jax.ShapeDtypeStruct((1, W, SRC), BF16)...  92.9 us
    unnamed x7, local copies, waits for them, and re-layouts  3.65 us

profile of v1, /device:TPU:1, one launch (start us, length us, event | category | flops | bytes accessed | tf_op | source)
XLA Modules:
  0.0 97.9 jit_solution(6292829357835932966)
XLA Ops:
  1.3 92.9 %forward_substitution.1 = (bf16[1,1024,512]{2,1,0:T(8,128)(2,1)}, bf16[2,32,512]{2,1,0:T(8,128)(2,1)}, bf16[2,128,512]{2,1,0:T(8,128)(2,1)}) custom-call(bf16[1,1024,1024]{2,1,0:T(8,128)(2,1)} %li.1, bf16[1,1024,512]{2,1,0:T(8,128)(2,1)} %rhs.1, bf16[1,1024,1024]{2,1,0:T(8,128)(2,1)} %tiles.1, bf16[2,32,1024]{2,1,0:T(8,128)(2,1)} %bitcast.2, ...), custom_call_target="tpu_custom_call" | custom-call | flops 2700000000 | bytes 8000000 | tf_op jit(solution)/shard_map/forward_substitution/pallas_call | solution.py:313
  94.2 0.0 copy-start.1
  94.2 0.0 copy-start
  94.3 2.3 %copy.16 = bf16[1,1024,512]{2,1,0:T(8,128)(2,1)} copy(bf16[1,1024,512]{2,1,0:T(8,128)(2,1)} %get-tuple-element.6) | data formatting | bytes 2097152
  96.6 0.0 copy-done.1
  96.6 0.6 copy.17
  97.2 0.0 copy-done
  97.2 0.7 copy.18
Async XLA Ops:
  94.2 2.3 %copy-start.1 = (bf16[2,32,512]{2,1,0:T(8,128)(2,1)S(1)}, bf16[2,32,512]{2,1,0:T(8,128)(2,1)}, u32[]{:S(2)}) copy-start(bf16[2,32,512]{2,1,0:T(8,128)(2,1)} %get-tuple-element.7) | copy-start | bytes 196612
  94.2 3.0 %copy-start = (bf16[2,128,512]{2,1,0:T(8,128)(2,1)S(1)}, bf16[2,128,512]{2,1,0:T(8,128)(2,1)}, u32[]{:S(2)}) copy-start(bf16[2,128,512]{2,1,0:T(8,128)(2,1)} %get-tuple-element.8) | copy-start | bytes 786436

commit v2 on v1

v2 whole, which is shorter than its diff:
```python
import functools
import jax
import jax.numpy as jnp
from jax import lax
from jax.experimental import pallas as pl
from jax.experimental.pallas import tpu as pltpu
from jax.sharding import PartitionSpec as P

MESH = pl.DeviceIdType.MESH
NZ, NY, NX, NK = 8, 4, 4, 2
NC = NX * NK
W = 1024
SRC = 512
CH = W // NZ
CS = SRC // NY
CZ = CS // NZ
RB = 256
AHEAD = 3
ORDER = (4, 3, 5, 2, 6, 1, 7, 0)
F32 = jnp.float32
BF16 = jnp.bfloat16


def kernel(
    li, rhs, tiles, mi, mr, mt, ti, tr, tl,
    leaf_o, mid_o, top_o,
    liv, rv, tv, xv, usend, yrecv, up, down, rup, rdown, rbuf,
    mig, mtg, mrv, flag, flagr, tiv, trv, ybf,
    pbuf, p32, crecv, qbuf, xrecv, zsend, zrecv, trt, tall, fall, tsend, midb, topb,
    load_sem, own_sem, y_s, y_r, mi_s, mi_r, mt_s, mt_r, mr_s, mr_r, fl_s, fl_r,
    up_s, up_r, dn_s, dn_r, r_s, f_s, r_r, c_s, c_r, x_s, x_r, z_s, z_r, t_s, t_r, a_s, a_r, mo_s, mo_r, to_s, to_r,
):
    row = lax.axis_index("row")
    col = lax.axis_index("col")
    z, y = row // NY, row % NY
    x, k = col // NK, col % NK

    def at_y(other):
        return (z * NY + other, col)

    def at_z(other):
        return (other * NY + y, col)

    def at_c(other):
        return (row, other)

    def remote(src, dst, s, r, device):
        return pltpu.make_async_remote_copy(
            src_ref=src, dst_ref=dst, send_sem=s, recv_sem=r, device_id=device, device_id_type=MESH
        )

    y_peers = [(y + d) % NY for d in range(1, NY)]

    rbuf[...] = jnp.zeros_like(rbuf)
    barrier = pltpu.get_barrier_semaphore()
    for other in y_peers:
        pl.semaphore_signal(barrier, inc=1, device_id=at_y(other), device_id_type=MESH)
    for d in range(1, NZ):
        pl.semaphore_signal(barrier, inc=1, device_id=at_z((z + d) % NZ), device_id_type=MESH)
    for d in range(1, NC):
        pl.semaphore_signal(barrier, inc=1, device_id=at_c((col + d) % NC), device_id_type=MESH)

    loads = {}

    def load(name, src, dst):
        copy = pltpu.make_async_copy(src, dst, load_sem.at[len(loads)])
        copy.start()
        loads[name] = copy

    for i in range(W // RB):
        rows = slice(i * RB, (i + 1) * RB)
        load(f"r{i}", rhs.at[0, rows, :], rv.at[rows, :])
        load(f"l{i}", li.at[0, rows, : (i + 1) * RB], liv.at[rows, : (i + 1) * RB])
    for i in range(W // RB):
        rows = slice(i * RB, (i + 1) * RB)
        load(f"t{i}", tiles.at[0, rows, :], tv.at[rows, :])
    own_cols = pl.ds(pl.multiple_of(y * CS, CS), CS)
    own_rows = pl.ds(pl.multiple_of(y * 32, 32), 32)
    load("mi", mi, mig.at[y])
    load("mr", mr.at[:, :, own_cols], mrv.at[:, own_rows, :])
    load("mt", mt, mtg.at[y])
    load("ti", ti, tiv)
    load("tr", tr.at[:, :, own_cols], trv)

    flag[...] = jnp.full(flag.shape, tl[0, 0].astype(F32))

    for i in range(W // RB):
        rows = slice(i * RB, (i + 1) * RB)
        loads[f"r{i}"].wait()
        loads[f"l{i}"].wait()
        xv[rows, :] = jnp.dot(
            liv[rows, : (i + 1) * RB], rv[: (i + 1) * RB, :], preferred_element_type=F32
        ).astype(BF16)
    leaf_copy = pltpu.make_async_copy(xv, leaf_o.at[0], own_sem.at[0])
    leaf_copy.start()

    pl.semaphore_wait(barrier, NY + NZ + NC - 3)

    sends = []

    def start(copy):
        copy.start()
        sends.append(copy)
        return copy

    fl_copies, mr_copies = [], []
    for n, other in enumerate(y_peers):
        fl_copies.append(start(remote(flag, flagr.at[n], fl_s.at[n], fl_r.at[n], at_y(other))))
        cols = pl.ds(pl.multiple_of(other * CS, CS), CS)
        mr_copies.append(
            start(remote(mr.at[:, :, cols], mrv.at[:, own_rows, :], mr_s.at[n], mr_r.at[n], at_y(other)))
        )

    def mi_copy(n):
        return remote(mi, mig.at[y], mi_s.at[n], mi_r.at[n], at_y(y_peers[n]))

    def mt_copy(n):
        return remote(mt, mtg.at[y], mt_s.at[n], mt_r.at[n], at_y(y_peers[n]))

    def u_copy(j, n):
        return remote(
            usend.at[j, y_peers[n]], yrecv.at[n, j], y_s.at[n, j], y_r.at[n, j], at_y(y_peers[n])
        )

    for i in range(W // RB):
        loads[f"t{i}"].wait()
    for o in range(NZ):
        chunk_rows = pl.ds(pl.multiple_of((z + ORDER[o]) % NZ * CH, CH), CH)
        update = jnp.dot(tv[chunk_rows, :], xv[...], preferred_element_type=F32).astype(BF16)
        for s in range(NY):
            usend[o, s] = update[:, s * CS : (s + 1) * CS]
        if o < AHEAD:
            for n in (1, 0, 2):
                start(u_copy(o, n))

    above, below = at_z((z + 1) % NZ), at_z((z + NZ - 1) % NZ)

    def up_copy(step):
        part = pl.ds(0, 1 if step == 0 else 2)
        return remote(
            up.at[step, part], rup.at[step, part], up_s.at[step], up_r.at[step], above
        )

    def down_copy(step):
        part = pl.ds(1, 1) if step == 0 else pl.ds(0, 2)
        return remote(
            down.at[step, part], rdown.at[step, part], dn_s.at[step], dn_r.at[step], below
        )

    def r_copy(step):
        part = rbuf.at[:, pl.ds(pl.multiple_of(z * CH, CH), CH), :]
        return remote(part, part, r_s.at[step], r_r.at[z], at_z(z + step))

    def f_copy(step):
        part = rbuf.at[:, pl.ds(pl.multiple_of((z - 2) * CH, CH), CH), :]
        return remote(part, part, f_s.at[step], r_r.at[z - 2], at_z(z + step))

    def r_wait(other):
        part = rbuf.at[:, pl.ds(pl.multiple_of(other * CH, CH), CH), :]
        remote(part, part, r_s.at[0], r_r.at[other], at_z(other)).wait_recv()

    for copy in fl_copies:
        copy.wait_recv()
    loads["mr"].wait()
    for copy in mr_copies:
        copy.wait_recv()

    def summed(o):
        parts = [(usend[o, y].astype(F32), flag[0:1, :] > 0.5)]
        for n in range(NY - 1):
            u_copy(o, n).wait_recv()
            parts.append((yrecv[n, o].astype(F32), flagr[n, 0:1, :] > 0.5))
        if o + AHEAD < NZ:
            for n in (1, 0, 2):
                start(u_copy(o + AHEAD, n))
        one = sum(jnp.where(f, u, 0.0) for u, f in parts)
        zero = sum(jnp.where(f, 0.0, u) for u, f in parts)
        return zero, one

    zero, one = summed(0)
    up[0, 0] = zero.astype(BF16)
    down[0, 1] = one.astype(BF16)
    start(up_copy(0))
    start(down_copy(0))
    for step in range(1, NZ // 2):
        zero, one = summed(2 * step - 1)
        up_copy(step - 1).wait_recv()
        if step > 1:
            one += rup[step - 1, 1].astype(F32)
        up[step, 0] = (zero + rup[step - 1, 0].astype(F32)).astype(BF16)
        up[step, 1] = one.astype(BF16)
        start(up_copy(step))
        zero, one = summed(2 * step)
        down_copy(step - 1).wait_recv()
        if step > 1:
            zero += rdown[step - 1, 0].astype(F32)
        down[step, 0] = zero.astype(BF16)
        down[step, 1] = (one + rdown[step - 1, 1].astype(F32)).astype(BF16)
        start(down_copy(step))
    both = summed(NZ - 1)
    up_copy(NZ // 2 - 1).wait_recv()
    down_copy(NZ // 2 - 1).wait_recv()
    mine = pl.ds(pl.multiple_of(z * CH, CH), CH)
    for b in range(2):
        total = both[b] + rup[NZ // 2 - 1, b].astype(F32) + rdown[NZ // 2 - 1, b].astype(F32)
        rbuf[b, mine, :] = (mrv[b].astype(F32) - total).astype(BF16)
    for step in (2, 1, 7, 6, 5):

        @pl.when(z + step < NZ)
        def _():
            r_copy(step).start()

    for n in (1, 0, 2):
        start(mi_copy(n))
    for n in (1, 0, 2):
        start(mt_copy(n))

    @pl.when(z >= 2)
    def _():
        r_wait(z - 2)
        for step in (2, 1):

            @pl.when(z + step < NZ)
            def _():
                f_copy(step).start()

    loads["mi"].wait()
    for n in range(NY - 1):
        mi_copy(n).wait_recv()
    for other in range(NZ - 1):

        @pl.when((other < z) & (other != z - 2))
        def _():
            r_wait(other)

    turned = []
    for b in range(2):
        solved = jnp.dot(mig[:, b].reshape(CH, W), rbuf[b], preferred_element_type=F32)
        ybf[b] = solved.astype(BF16)
        turned.append(solved.T.astype(BF16))

    loads["mt"].wait()
    for n in range(NY - 1):
        mt_copy(n).wait_recv()
    for b in range(2):
        update = jnp.dot(turned[b], mtg[:, b].reshape(CH, W), preferred_element_type=F32)
        for c in range(NC):
            p32[c % NK, c // NK, b] = update[:, c * CH : (c + 1) * CH]
    pbuf[...] = p32[1 - k].astype(BF16)
    core_copy = start(
        remote(pbuf, crecv, c_s.at[0], c_r.at[0], at_c(x * NK + 1 - k))
    )

    mid_copies = []
    for n, other in enumerate(y_peers):
        rows = pl.ds(pl.multiple_of(other * 32, 32), 32)
        mid_copies.append(start(remote(ybf.at[:, rows, :], midb.at[n], mo_s.at[n], mo_r.at[n], at_y(other))))
    mid_copy = pltpu.make_async_copy(ybf.at[:, own_rows, :], mid_o.at[:, :, own_cols], own_sem.at[1])
    mid_copy.start()

    loads["tr"].wait()
    for b in range(2):
        trt[b] = trv[b].astype(F32).T

    core_copy.wait_recv()
    x_copies = []
    for n in range(NX - 1):
        other = (x + n + 1) % NX
        qbuf[n] = (p32[k, other] + crecv[other].astype(F32)).astype(BF16)
        x_copies.append(
            start(remote(qbuf.at[n], xrecv.at[n], x_s.at[n], x_r.at[n], at_c(other * NK + k)))
        )
    total = p32[k, x] + crecv[x].astype(F32)
    for n in range(NX - 1):
        x_copies[n].wait_recv()
        total += xrecv[n].astype(F32)
    for other in range(NZ):
        zsend[other] = total[:, other * CZ : (other + 1) * CZ, :].astype(BF16)
    my_cols = pl.ds(pl.multiple_of(z * CZ, CZ), CZ)
    for d in range(1, NZ):
        other = (z + d) % NZ
        start(remote(zsend.at[other], zrecv.at[z], z_s.at[d - 1], z_r.at[z], at_z(other)))
    total = zsend[z].astype(F32)
    for d in range(1, NZ):
        other = (z + d) % NZ
        remote(zrecv.at[other], zrecv.at[other], z_s.at[d - 1], z_r.at[other], at_z(other)).wait_recv()
        total += zrecv[other].astype(F32)

    tall[col] = (trt[:, my_cols, :] - total).astype(BF16)
    for d in range(1, NC):
        other = (col + d) % NC
        start(remote(tall.at[col], tall.at[col], t_s.at[d - 1], t_r.at[col], at_c(other)))
    loads["ti"].wait()
    for d in range(1, NC):
        other = (col + d) % NC
        remote(tall.at[other], tall.at[other], t_s.at[d - 1], t_r.at[other], at_c(other)).wait_recv()

    for b in range(2):
        resid = jnp.concatenate([tall[c, b] for c in range(NC)], axis=1)
        fall[z, b] = jnp.dot(resid, tiv[b], preferred_element_type=F32).astype(BF16)
    for d in range(1, NZ):
        other = (z + d) % NZ
        start(remote(fall.at[z], fall.at[z], a_s.at[d - 1], a_r.at[z], at_z(other)))
    for d in range(1, NZ):
        other = (z + d) % NZ
        remote(fall.at[other], fall.at[other], a_s.at[d - 1], a_r.at[other], at_z(other)).wait_recv()
    for b in range(2):
        tsend[b] = fall[:, b].reshape(CS, CH).astype(F32).T.astype(BF16)
    top_copies = []
    for n, other in enumerate(y_peers):
        top_copies.append(start(remote(tsend, topb.at[n], to_s.at[n], to_r.at[n], at_y(other))))
    outs = [leaf_copy, mid_copy]

    def write(src, dst):
        copy = pltpu.make_async_copy(src, dst, own_sem.at[len(outs)])
        copy.start()
        outs.append(copy)

    write(tsend, top_o.at[:, :, own_cols])
    for n in range(NY - 1):
        cols = pl.ds(pl.multiple_of((y + NY - 1 - n) % NY * CS, CS), CS)
        mid_copies[n].wait_recv()
        write(midb.at[n], mid_o.at[:, :, cols])
    for n in (0, 2, 1):
        cols = pl.ds(pl.multiple_of((y + NY - 1 - n) % NY * CS, CS), CS)
        top_copies[n].wait_recv()
        write(topb.at[n], top_o.at[:, :, cols])

    for step in (7, 6, 5, 2, 1):

        @pl.when(z + step < NZ)
        def _():
            r_copy(step).wait_send()

    for step in (2, 1):

        @pl.when((z >= 2) & (z + step < NZ))
        def _():
            f_copy(step).wait_send()

    for copy in sends:
        copy.wait_send()
    for copy in outs:
        copy.wait()


def hand_over(a, b, c, a_o, b_o, c_o, a_v, b_v, c_v, sem):
    rows = W // 4
    moves = [(a.at[0, pl.ds(i * rows, rows)], a_v.at[pl.ds(i * rows, rows)], a_o.at[0, pl.ds(i * rows, rows)]) for i in range(4)]
    moves += [(c, c_v, c_o), (b, b_v, b_o)]
    ins = [pltpu.make_async_copy(src, via, sem.at[0, i]) for i, (src, via, dst) in enumerate(moves)]
    outs = [pltpu.make_async_copy(via, dst, sem.at[1, i]) for i, (src, via, dst) in enumerate(moves)]
    for copy in ins:
        copy.start()
    for i, copy in enumerate(ins):
        copy.wait()
        outs[i].start()
    for copy in outs:
        copy.wait()


def local(li, rhs, tiles, mi, mr, mt, ti, tr, tl):
    dma = pltpu.SemaphoreType.DMA
    vmem = pltpu.VMEM
    any_spec = pl.BlockSpec(memory_space=pl.ANY)
    n = NY - 1
    parts = pl.pallas_call(
        kernel,
        out_shape=(
            jax.ShapeDtypeStruct((1, W, SRC), BF16),
            jax.ShapeDtypeStruct((2, 32, SRC), BF16),
            jax.ShapeDtypeStruct((2, CH, SRC), BF16),
        ),
        in_specs=[pl.BlockSpec(memory_space=pltpu.HBM)] * 8 + [pl.BlockSpec(memory_space=pltpu.SMEM)],
        out_specs=(any_spec,) * 3,
        scratch_shapes=[
            vmem((W, W), BF16),
            vmem((W, SRC), BF16),
            vmem((W, W), BF16),
            vmem((W, SRC), BF16),
            vmem((NZ, NY, CH, CS), BF16),
            vmem((n, NZ, CH, CS), BF16),
            vmem((NZ // 2, 2, CH, CS), BF16),
            vmem((NZ // 2, 2, CH, CS), BF16),
            vmem((NZ // 2, 2, CH, CS), BF16),
            vmem((NZ // 2, 2, CH, CS), BF16),
            vmem((2, W, CS), BF16),
            vmem((NY, 2, 32, W), BF16),
            vmem((NY, 2, 32, W), BF16),
            vmem((2, CH, CS), BF16),
            vmem((8, 128), F32),
            vmem((n, 8, 128), F32),
            vmem((2, W, CH), BF16),
            vmem((2, CH, CS), BF16),
            vmem((2, CH, CS), BF16),
            vmem((NX, 2, CS, CH), BF16),
            vmem((NK, NX, 2, CS, CH), F32),
            vmem((NX, 2, CS, CH), BF16),
            vmem((NX - 1, 2, CS, CH), BF16),
            vmem((NX - 1, 2, CS, CH), BF16),
            vmem((NZ, 2, CZ, CH), BF16),
            vmem((NZ, 2, CZ, CH), BF16),
            vmem((2, CS, CH), F32),
            vmem((NC, 2, CZ, CH), BF16),
            vmem((NZ, 2, CZ, CH), BF16),
            vmem((2, CH, CS), BF16),
            vmem((n, 2, 32, CS), BF16),
            vmem((n, 2, CH, CS), BF16),
            dma((17,)), dma((9,)),
            dma((n, NZ)), dma((n, NZ)),
            dma((n,)), dma((n,)), dma((n,)), dma((n,)),
            dma((n,)), dma((n,)), dma((n,)), dma((n,)),
            dma((NZ // 2,)), dma((NZ // 2,)), dma((NZ // 2,)), dma((NZ // 2,)),
            dma((NZ,)), dma((3,)), dma((NZ,)),
            dma((1,)), dma((1,)), dma((NX - 1,)), dma((NX - 1,)),
            dma((NZ - 1,)), dma((NZ,)), dma((NC - 1,)), dma((NC,)),
            dma((NZ - 1,)), dma((NZ,)),
            dma((n,)), dma((n,)), dma((n,)), dma((n,)),
        ],
        compiler_params=pltpu.CompilerParams(
            collective_id=0, has_side_effects=True, vmem_limit_bytes=56 * 1024 * 1024
        ),
        cost_estimate=pl.CostEstimate(flops=2_700_000_000, bytes_accessed=8_000_000, transcendentals=0),
        name="forward_substitution",
    )(li, rhs, tiles, jnp.swapaxes(mi, 1, 2), mr, jnp.swapaxes(mt, 1, 2), ti, tr, tl)
    return pl.pallas_call(
        hand_over,
        out_shape=tuple(jax.ShapeDtypeStruct(part.shape, part.dtype) for part in parts),
        in_specs=[any_spec] * 3,
        out_specs=(any_spec,) * 3,
        scratch_shapes=[vmem((W, SRC), BF16), vmem((2, 32, SRC), BF16), vmem((2, CH, SRC), BF16), dma((2, 6))],
        name="results",
    )(*parts)


def solution(mesh):
    placed = (
        P(("row", "col"), None, None),
        P(("row", "col"), None, None),
        P(("row", "col"), None, None),
        P("col", None, "row"),
        P("col", "row", None),
        P("col", None, "row"),
        P(None, None, "col"),
        P(None, "col", None),
        P(("row", "col"), None),
    )
    return jax.shard_map(
        local,
        mesh=mesh,
        in_specs=placed,
        out_specs=(P(("row", "col"), None, None), P("col", "row", None), P(None, "col", None)),
        check_vma=False,
    )
```

time: 99.2 us -> 70.1 us (0.71); the launches traced: 97.9 us -> 70 us
  Pallas kernels: 92.9 us -> 68.7 us
  local copies, waits for them, and re-layouts: 3.65 us -> 0 us
    pallas_call x1, Pallas kernels: 92.9 us -> 66.6 us  [local(): pl.pallas_call(kernel, out_shape=(jax.ShapeDtypeStruct((1, W, SRC), BF16)...]
    unnamed x7 -> x0, local copies, waits for them, and re-layouts: 3.65 us -> none
    pallas_call x0 -> x1, Pallas kernels: none -> 2.12 us  [local(): pl.pallas_call(hand_over, out_shape=tuple((jax.ShapeDtypeStruct(part.shap...]
where the time goes in v2:
time: 70.1 us; the launch traced here: 70 us
  Pallas kernels  68.7 us (98%)
  between operations  1.29 us (2%)
    pallas_call x1, Pallas kernels, local(): pl.pallas_call(kernel, out_shape=(jax.ShapeDtypeStruct((1, W, SRC), BF16)...  66.6 us
    pallas_call x1, Pallas kernels, local(): pl.pallas_call(hand_over, out_shape=tuple((jax.ShapeDtypeStruct(part.shap...  2.12 us

profile of v2, /device:TPU:1, one launch (start us, length us, event | category | flops | bytes accessed | tf_op | source)
XLA Modules:
  0.0 70.0 jit_solution(18230354248519952794)
XLA Ops:
  1.3 66.6 %forward_substitution.1 = (bf16[1,1024,512]{2,1,0:T(8,128)(2,1)}, bf16[2,32,512]{2,1,0:T(8,128)(2,1)}, bf16[2,128,512]{2,1,0:T(8,128)(2,1)}) custom-call(bf16[1,1024,1024]{2,1,0:T(8,128)(2,1)} %li.1, bf16[1,1024,512]{2,1,0:T(8,128)(2,1)} %rhs.1, bf16[1,1024,1024]{2,1,0:T(8,128)(2,1)} %tiles.1, bf16[2,32,1024]{2,1,0:T(8,128)(2,1)} %bitcast.2, ...), custom_call_target="tpu_custom_call" | custom-call | flops 2700000000 | bytes 8000000 | tf_op jit(solution)/shard_map/forward_substitution/pallas_call | solution.py:367
  67.8 2.1 %results.1 = (bf16[1,1024,512]{2,1,0:T(8,128)(2,1)}, bf16[2,32,512]{2,1,0:T(8,128)(2,1)}, bf16[2,128,512]{2,1,0:T(8,128)(2,1)}) custom-call(bf16[1,1024,512]{2,1,0:T(8,128)(2,1)} %get-tuple-element.6.a, bf16[2,32,512]{2,1,0:T(8,128)(2,1)} %get-tuple-element.7.b, bf16[2,128,512]{2,1,0:T(8,128)(2,1)} %get-tuple-element.8.c), custom_call_target="tpu_custom_call" | custom-call | tf_op jit(solution)/shard_map/results/pallas_call | solution.py:426

commit v3 on v2

--- a/solution.py
+++ b/solution.py
@@ -26,7 +26,7 @@
     leaf_o, mid_o, top_o,
     liv, rv, tv, xv, usend, yrecv, up, down, rup, rdown, rbuf,
     mig, mtg, mrv, flag, flagr, tiv, trv, ybf,
-    pbuf, p32, crecv, qbuf, xrecv, zsend, zrecv, trt, tall, fall, tsend, midb, topb,
+    pbuf, p32, crecv, qbuf, xrecv, zsend, zrecv, trt, tall, fall,
     load_sem, own_sem, y_s, y_r, mi_s, mi_r, mt_s, mt_r, mr_s, mr_r, fl_s, fl_r,
     up_s, up_r, dn_s, dn_r, r_s, f_s, r_r, c_s, c_r, x_s, x_r, z_s, z_r, t_s, t_r, a_s, a_r, mo_s, mo_r, to_s, to_r,
 ):
@@ -242,40 +242,48 @@
     loads["mt"].wait()
     for n in range(NY - 1):
         mt_copy(n).wait_recv()
+    core_copies = []
     for b in range(2):
         update = jnp.dot(turned[b], mtg[:, b].reshape(CH, W), preferred_element_type=F32)
         for c in range(NC):
-            p32[c % NK, c // NK, b] = update[:, c * CH : (c + 1) * CH]
-    pbuf[...] = p32[1 - k].astype(BF16)
-    core_copy = start(
-        remote(pbuf, crecv, c_s.at[0], c_r.at[0], at_c(x * NK + 1 - k))
-    )
+            p32[c % NK, b, c // NK] = update[:, c * CH : (c + 1) * CH]
+        pbuf[b] = p32[1 - k, b].astype(BF16)
+        core_copies.append(
+            start(remote(pbuf.at[b], crecv.at[b], c_s.at[b], c_r.at[b], at_c(x * NK + 1 - k)))
+        )
 
     mid_copies = []
     for n, other in enumerate(y_peers):
         rows = pl.ds(pl.multiple_of(other * 32, 32), 32)
-        mid_copies.append(start(remote(ybf.at[:, rows, :], midb.at[n], mo_s.at[n], mo_r.at[n], at_y(other))))
-    mid_copy = pltpu.make_async_copy(ybf.at[:, own_rows, :], mid_o.at[:, :, own_cols], own_sem.at[1])
+        mid_copies.append(start(remote(ybf.at[:, rows, :], mid_o.at[y], mo_s.at[n], mo_r.at[n], at_y(other))))
+    mid_copy = pltpu.make_async_copy(ybf.at[:, own_rows, :], mid_o.at[y], own_sem.at[1])
     mid_copy.start()
 
     loads["tr"].wait()
     for b in range(2):
         trt[b] = trv[b].astype(F32).T
 
-    core_copy.wait_recv()
     x_copies = []
-    for n in range(NX - 1):
-        other = (x + n + 1) % NX
-        qbuf[n] = (p32[k, other] + crecv[other].astype(F32)).astype(BF16)
-        x_copies.append(
-            start(remote(qbuf.at[n], xrecv.at[n], x_s.at[n], x_r.at[n], at_c(other * NK + k)))
-        )
-    total = p32[k, x] + crecv[x].astype(F32)
-    for n in range(NX - 1):
-        x_copies[n].wait_recv()
-        total += xrecv[n].astype(F32)
+    sums = []
+    for b in range(2):
+        core_copies[b].wait_recv()
+        for n in range(NX - 1):
+            other = (x + n + 1) % NX
+            qbuf[b, n] = (p32[k, b, other] + crecv[b, other].astype(F32)).astype(BF16)
+            x_copies.append(
+                start(
+                    remote(qbuf.at[b, n], xrecv.at[b, n], x_s.at[b, n], x_r.at[b, n], at_c(other * NK + k))
+                )
+            )
+        sums.append(p32[k, b, x] + crecv[b, x].astype(F32))
+    for b in range(2):
+        for n in range(NX - 1):
+            x_copies[b * (NX - 1) + n].wait_recv()
+            sums[b] += xrecv[b, n].astype(F32)
+
     for other in range(NZ):
-        zsend[other] = total[:, other * CZ : (other + 1) * CZ, :].astype(BF16)
+        for b in range(2):
+            zsend[other, b] = sums[b][other * CZ : (other + 1) * CZ, :].astype(BF16)
     my_cols = pl.ds(pl.multiple_of(z * CZ, CZ), CZ)
     for d in range(1, NZ):
         other = (z + d) % NZ
@@ -301,30 +309,27 @@
     for d in range(1, NZ):
         other = (z + d) % NZ
         start(remote(fall.at[z], fall.at[z], a_s.at[d - 1], a_r.at[z], at_z(other)))
-    for d in range(1, NZ):
+    outs = [leaf_copy, mid_copy]
+    to_copies = []
+
+    def pass_on(at, slot):
+        for n in (1, 0, 2):
+            to_copies.append(
+                start(
+                    remote(
+                        fall.at[at], top_o.at[y, at], to_s.at[n, slot], to_r.at[n, at], at_y(y_peers[n])
+                    )
+                )
+            )
+        copy = pltpu.make_async_copy(fall.at[at], top_o.at[y, at], own_sem.at[2 + slot])
+        copy.start()
+        outs.append(copy)
+
+    pass_on(z, 0)
+    for slot, d in enumerate((1, 7, 2, 6, 3, 5, 4)):
         other = (z + d) % NZ
         remote(fall.at[other], fall.at[other], a_s.at[d - 1], a_r.at[other], at_z(other)).wait_recv()
-    for b in range(2):
-        tsend[b] = fall[:, b].reshape(CS, CH).astype(F32).T.astype(BF16)
-    top_copies = []
-    for n, other in enumerate(y_peers):
-        top_copies.append(start(remote(tsend, topb.at[n], to_s.at[n], to_r.at[n], at_y(other))))
-    outs = [leaf_copy, mid_copy]
-
-    def write(src, dst):
-        copy = pltpu.make_async_copy(src, dst, own_sem.at[len(outs)])
-        copy.start()
-        outs.append(copy)
-
-    write(tsend, top_o.at[:, :, own_cols])
-    for n in range(NY - 1):
-        cols = pl.ds(pl.multiple_of((y + NY - 1 - n) % NY * CS, CS), CS)
-        mid_copies[n].wait_recv()
-        write(midb.at[n], mid_o.at[:, :, cols])
-    for n in (0, 2, 1):
-        cols = pl.ds(pl.multiple_of((y + NY - 1 - n) % NY * CS, CS), CS)
-        top_copies[n].wait_recv()
-        write(topb.at[n], top_o.at[:, :, cols])
+        pass_on(other, slot + 1)
 
     for step in (7, 6, 5, 2, 1):
 
@@ -342,20 +347,43 @@
         copy.wait_send()
     for copy in outs:
         copy.wait()
-
-
-def hand_over(a, b, c, a_o, b_o, c_o, a_v, b_v, c_v, sem):
+    for n in range(NY - 1):
+        mid_copies[n].wait_recv()
+    for copy in to_copies:
+        copy.wait_recv()
+
+
+def hand_over(leaf, mid, top, leaf_o, mid_o, top_o, leaf_v, mid_v, raw_v, top_v, sem):
     rows = W // 4
-    moves = [(a.at[0, pl.ds(i * rows, rows)], a_v.at[pl.ds(i * rows, rows)], a_o.at[0, pl.ds(i * rows, rows)]) for i in range(4)]
-    moves += [(c, c_v, c_o), (b, b_v, b_o)]
-    ins = [pltpu.make_async_copy(src, via, sem.at[0, i]) for i, (src, via, dst) in enumerate(moves)]
-    outs = [pltpu.make_async_copy(via, dst, sem.at[1, i]) for i, (src, via, dst) in enumerate(moves)]
-    for copy in ins:
+    parts = [pl.ds(i * rows, rows) for i in range(4)]
+    load_top = pltpu.make_async_copy(top, raw_v, sem.at[0, 0])
+    load_mid = [
+        pltpu.make_async_copy(mid.at[i], mid_v.at[:, :, i * CS : (i + 1) * CS], sem.at[0, 1 + i]) for i in range(NY)
+    ]
+    load_leaf = [
+        pltpu.make_async_copy(leaf.at[0, part], leaf_v.at[part], sem.at[0, 1 + NY + i])
+        for i, part in enumerate(parts)
+    ]
+    stores = [
+        pltpu.make_async_copy(leaf_v.at[part], leaf_o.at[0, part], sem.at[1, i]) for i, part in enumerate(parts)
+    ]
+    store_mid = pltpu.make_async_copy(mid_v, mid_o, sem.at[1, 4])
+    store_top = pltpu.make_async_copy(top_v, top_o, sem.at[1, 5])
+    for copy in [load_top] + load_leaf + load_mid:
         copy.start()
-    for i, copy in enumerate(ins):
+    load_top.wait()
+    for i in range(NY):
+        for b in range(2):
+            block = raw_v[i, :, b].reshape(CS, CH).astype(F32)
+            top_v[b, :, i * CS : (i + 1) * CS] = block.T.astype(BF16)
+    store_top.start()
+    for load, store in zip(load_leaf, stores):
+        load.wait()
+        store.start()
+    for copy in load_mid:
         copy.wait()
-        outs[i].start()
-    for copy in outs:
+    store_mid.start()
+    for copy in stores + [store_mid, store_top]:
         copy.wait()
 
 
@@ -368,8 +396,8 @@
         kernel,
         out_shape=(
             jax.ShapeDtypeStruct((1, W, SRC), BF16),
-            jax.ShapeDtypeStruct((2, 32, SRC), BF16),
-            jax.ShapeDtypeStruct((2, CH, SRC), BF16),
+            jax.ShapeDtypeStruct((NY, 2, 32, CS), BF16),
+            jax.ShapeDtypeStruct((NY, NZ, 2, CZ, CH), BF16),
         ),
         in_specs=[pl.BlockSpec(memory_space=pltpu.HBM)] * 8 + [pl.BlockSpec(memory_space=pltpu.SMEM)],
         out_specs=(any_spec,) * 3,
@@ -393,29 +421,26 @@
             vmem((2, W, CH), BF16),
             vmem((2, CH, CS), BF16),
             vmem((2, CH, CS), BF16),
-            vmem((NX, 2, CS, CH), BF16),
-            vmem((NK, NX, 2, CS, CH), F32),
-            vmem((NX, 2, CS, CH), BF16),
-            vmem((NX - 1, 2, CS, CH), BF16),
-            vmem((NX - 1, 2, CS, CH), BF16),
+            vmem((2, NX, CS, CH), BF16),
+            vmem((NK, 2, NX, CS, CH), F32),
+            vmem((2, NX, CS, CH), BF16),
+            vmem((2, NX - 1, CS, CH), BF16),
+            vmem((2, NX - 1, CS, CH), BF16),
             vmem((NZ, 2, CZ, CH), BF16),
             vmem((NZ, 2, CZ, CH), BF16),
             vmem((2, CS, CH), F32),
             vmem((NC, 2, CZ, CH), BF16),
             vmem((NZ, 2, CZ, CH), BF16),
-            vmem((2, CH, CS), BF16),
-            vmem((n, 2, 32, CS), BF16),
-            vmem((n, 2, CH, CS), BF16),
-            dma((17,)), dma((9,)),
+            dma((17,)), dma((2 + NZ,)),
             dma((n, NZ)), dma((n, NZ)),
             dma((n,)), dma((n,)), dma((n,)), dma((n,)),
             dma((n,)), dma((n,)), dma((n,)), dma((n,)),
             dma((NZ // 2,)), dma((NZ // 2,)), dma((NZ // 2,)), dma((NZ // 2,)),
             dma((NZ,)), dma((3,)), dma((NZ,)),
-            dma((1,)), dma((1,)), dma((NX - 1,)), dma((NX - 1,)),
+            dma((2,)), dma((2,)), dma((2, NX - 1)), dma((2, NX - 1)),
             dma((NZ - 1,)), dma((NZ,)), dma((NC - 1,)), dma((NC,)),
             dma((NZ - 1,)), dma((NZ,)),
-            dma((n,)), dma((n,)), dma((n,)), dma((n,)),
+            dma((n,)), dma((n,)), dma((n, NZ)), dma((n, NZ)),
         ],
         compiler_params=pltpu.CompilerParams(
             collective_id=0, has_side_effects=True, vmem_limit_bytes=56 * 1024 * 1024
@@ -425,10 +450,20 @@
     )(li, rhs, tiles, jnp.swapaxes(mi, 1, 2), mr, jnp.swapaxes(mt, 1, 2), ti, tr, tl)
     return pl.pallas_call(
         hand_over,
-        out_shape=tuple(jax.ShapeDtypeStruct(part.shape, part.dtype) for part in parts),
+        out_shape=(
+            jax.ShapeDtypeStruct((1, W, SRC), BF16),
+            jax.ShapeDtypeStruct((2, 32, SRC), BF16),
+            jax.ShapeDtypeStruct((2, CH, SRC), BF16),
+        ),
         in_specs=[any_spec] * 3,
         out_specs=(any_spec,) * 3,
-        scratch_shapes=[vmem((W, SRC), BF16), vmem((2, 32, SRC), BF16), vmem((2, CH, SRC), BF16), dma((2, 6))],
+        scratch_shapes=[
+            vmem((W, SRC), BF16),
+            vmem((2, 32, SRC), BF16),
+            vmem((NY, NZ, 2, CZ, CH), BF16),
+            vmem((2, CH, SRC), BF16),
+            dma((2, 9)),
+        ],
         name="results",
     )(*parts)
 

time: 70.1 us -> 69.4 us (0.990)
    pallas_call x1, Pallas kernels: 66.6 us -> 65.7 us  [local(): pl.pallas_call(kernel, out_shape=(jax.ShapeDtypeStruct((1, W, SRC), BF16)...]
where the time goes in v3:
time: 69.4 us; the launch traced here: 69.3 us
  Pallas kernels  68 us (98%)
  between operations  1.29 us (2%)
    pallas_call x1, Pallas kernels, local(): pl.pallas_call(kernel, out_shape=(jax.ShapeDtypeStruct((1, W, SRC), BF16)...  65.7 us
    pallas_call x1, Pallas kernels, local(): pl.pallas_call(hand_over, out_shape=(jax.ShapeDtypeStruct((1, W, SRC), BF...  2.31 us

profile of v3, /device:TPU:1, one launch (start us, length us, event | category | flops | bytes accessed | tf_op | source)
XLA Modules:
  0.0 69.3 jit_solution(14406340193021414465)
XLA Ops:
  1.3 65.7 %forward_substitution.1 = (bf16[1,1024,512]{2,1,0:T(8,128)(2,1)}, bf16[4,2,32,128]{3,2,1,0:T(8,128)(2,1)}, bf16[4,8,2,16,128]{4,3,2,1,0:T(8,128)(2,1)}) custom-call(bf16[1,1024,1024]{2,1,0:T(8,128)(2,1)} %li.1, bf16[1,1024,512]{2,1,0:T(8,128)(2,1)} %rhs.1, bf16[1,1024,1024]{2,1,0:T(8,128)(2,1)} %tiles.1, bf16[2,32,1024]{2,1,0:T(8,128)(2,1)} %bitcast.2, ...), custom_call_target="tpu_custom_call" | custom-call | flops 2700000000 | bytes 8000000 | tf_op jit(solution)/shard_map/forward_substitution/pallas_call | solution.py:395
  67.0 2.3 %results.1 = (bf16[1,1024,512]{2,1,0:T(8,128)(2,1)}, bf16[2,32,512]{2,1,0:T(8,128)(2,1)}, bf16[2,128,512]{2,1,0:T(8,128)(2,1)}) custom-call(bf16[1,1024,512]{2,1,0:T(8,128)(2,1)} %get-tuple-element.6.leaf, bf16[4,2,32,128]{3,2,1,0:T(8,128)(2,1)} %get-tuple-element.7.mid, bf16[4,8,2,16,128]{4,3,2,1,0:T(8,128)(2,1)} %get-tuple-element.8.top), custom_call_target="tpu_custom_call" | custom-call | tf_op jit(solution)/shard_map/results/pallas_call | solution.py:451

commit v4 on v3

--- a/solution.py
+++ b/solution.py
@@ -26,9 +26,9 @@
     leaf_o, mid_o, top_o,
     liv, rv, tv, xv, usend, yrecv, up, down, rup, rdown, rbuf,
     mig, mtg, mrv, flag, flagr, tiv, trv, ybf,
-    pbuf, p32, crecv, qbuf, xrecv, zsend, zrecv, trt, tall, fall,
+    pbuf, p32, crecv, qbuf, xrecv, trt, tall, fall,
     load_sem, own_sem, y_s, y_r, mi_s, mi_r, mt_s, mt_r, mr_s, mr_r, fl_s, fl_r,
-    up_s, up_r, dn_s, dn_r, r_s, f_s, r_r, c_s, c_r, x_s, x_r, z_s, z_r, t_s, t_r, a_s, a_r, mo_s, mo_r, to_s, to_r,
+    up_s, up_r, dn_s, dn_r, r_s, f_s, r_r, c_s, c_r, x_s, x_r, t_s, t_r, a_s, a_r, mo_s, mo_r, to_s, to_r, ring_in,
 ):
     row = lax.axis_index("row")
     col = lax.axis_index("col")
@@ -43,6 +43,9 @@
 
     def at_c(other):
         return (row, other)
+
+    def at_xz(other_x, other_z):
+        return (other_z * NY + y, other_x * NK + k)
 
     def remote(src, dst, s, r, device):
         return pltpu.make_async_remote_copy(
@@ -95,6 +98,9 @@
     leaf_copy.start()
 
     pl.semaphore_wait(barrier, NY + NZ + NC - 3)
+
+    for d in range(1, NX):
+        pl.semaphore_signal(ring_in, inc=1, device_id=at_c((x + d) % NX * NK + k), device_id_type=MESH)
 
     sends = []
 
@@ -263,36 +269,27 @@
     for b in range(2):
         trt[b] = trv[b].astype(F32).T
 
-    x_copies = []
-    sums = []
     for b in range(2):
         core_copies[b].wait_recv()
-        for n in range(NX - 1):
-            other = (x + n + 1) % NX
-            qbuf[b, n] = (p32[k, b, other] + crecv[b, other].astype(F32)).astype(BF16)
-            x_copies.append(
-                start(
-                    remote(qbuf.at[b, n], xrecv.at[b, n], x_s.at[b, n], x_r.at[b, n], at_c(other * NK + k))
-                )
-            )
-        sums.append(p32[k, b, x] + crecv[b, x].astype(F32))
-    for b in range(2):
-        for n in range(NX - 1):
-            x_copies[b * (NX - 1) + n].wait_recv()
-            sums[b] += xrecv[b, n].astype(F32)
-
-    for other in range(NZ):
-        for b in range(2):
-            zsend[other, b] = sums[b][other * CZ : (other + 1) * CZ, :].astype(BF16)
+        for other in range(NX):
+            part = (p32[k, b, other] + crecv[b, other].astype(F32)).astype(BF16)
+            for slot in range(NZ):
+                qbuf[other, slot, b] = part[slot * CZ : (slot + 1) * CZ, :]
+    steps = [(dx, dz) for dz in (4, 3, 5, 2, 6, 1, 7, 0) for dx in (2, 1, 3, 0) if dx or dz]
+    pl.semaphore_wait(ring_in, NX - 1)
+    for dx, dz in steps:
+        ox, oz = (x + dx) % NX, (z + dz) % NZ
+        start(
+            remote(qbuf.at[ox, oz], xrecv.at[x, z], x_s.at[dx, dz], x_r.at[x, z], at_xz(ox, oz))
+        )
+    total = qbuf[x, z].astype(F32)
+    for dx, dz in reversed(steps):
+        ox, oz = (x + dx) % NX, (z + dz) % NZ
+        remote(
+            xrecv.at[ox, oz], xrecv.at[ox, oz], x_s.at[dx, dz], x_r.at[ox, oz], at_xz(ox, oz)
+        ).wait_recv()
+        total += xrecv[ox, oz].astype(F32)
     my_cols = pl.ds(pl.multiple_of(z * CZ, CZ), CZ)
-    for d in range(1, NZ):
-        other = (z + d) % NZ
-        start(remote(zsend.at[other], zrecv.at[z], z_s.at[d - 1], z_r.at[z], at_z(other)))
-    total = zsend[z].astype(F32)
-    for d in range(1, NZ):
-        other = (z + d) % NZ
-        remote(zrecv.at[other], zrecv.at[other], z_s.at[d - 1], z_r.at[other], at_z(other)).wait_recv()
-        total += zrecv[other].astype(F32)
 
     tall[col] = (trt[:, my_cols, :] - total).astype(BF16)
     for d in range(1, NC):
@@ -424,10 +421,8 @@
             vmem((2, NX, CS, CH), BF16),
             vmem((NK, 2, NX, CS, CH), F32),
             vmem((2, NX, CS, CH), BF16),
-            vmem((2, NX - 1, CS, CH), BF16),
-            vmem((2, NX - 1, CS, CH), BF16),
-            vmem((NZ, 2, CZ, CH), BF16),
-            vmem((NZ, 2, CZ, CH), BF16),
+            vmem((NX, NZ, 2, CZ, CH), BF16),
+            vmem((NX, NZ, 2, CZ, CH), BF16),
             vmem((2, CS, CH), F32),
             vmem((NC, 2, CZ, CH), BF16),
             vmem((NZ, 2, CZ, CH), BF16),
@@ -437,10 +432,11 @@
             dma((n,)), dma((n,)), dma((n,)), dma((n,)),
             dma((NZ // 2,)), dma((NZ // 2,)), dma((NZ // 2,)), dma((NZ // 2,)),
             dma((NZ,)), dma((3,)), dma((NZ,)),
-            dma((2,)), dma((2,)), dma((2, NX - 1)), dma((2, NX - 1)),
-            dma((NZ - 1,)), dma((NZ,)), dma((NC - 1,)), dma((NC,)),
+            dma((2,)), dma((2,)), dma((NX, NZ)), dma((NX, NZ)),
+            dma((NC - 1,)), dma((NC,)),
             dma((NZ - 1,)), dma((NZ,)),
             dma((n,)), dma((n,)), dma((n, NZ)), dma((n, NZ)),
+            pltpu.SemaphoreType.REGULAR,
         ],
         compiler_params=pltpu.CompilerParams(
             collective_id=0, has_side_effects=True, vmem_limit_bytes=56 * 1024 * 1024

time: 69.4 us -> 68.2 us (0.983)
  Pallas kernels: 68 us -> 66.8 us
    pallas_call x1, Pallas kernels: 65.7 us -> 64.5 us  [local(): pl.pallas_call(kernel, out_shape=(jax.ShapeDtypeStruct((1, W, SRC), BF16)...]
where the time goes in v4:
time: 68.2 us; the launch traced here: 68.1 us
  Pallas kernels  66.8 us (98%)
  between operations  1.29 us (2%)
    pallas_call x1, Pallas kernels, local(): pl.pallas_call(kernel, out_shape=(jax.ShapeDtypeStruct((1, W, SRC), BF16)...  64.5 us
    pallas_call x1, Pallas kernels, local(): pl.pallas_call(hand_over, out_shape=(jax.ShapeDtypeStruct((1, W, SRC), BF...  2.31 us

profile of v4, /device:TPU:1, one launch (start us, length us, event | category | flops | bytes accessed | tf_op | source)
XLA Modules:
  0.0 68.1 jit_solution(12310459274504859993)
XLA Ops:
  1.3 64.5 %forward_substitution.1 = (bf16[1,1024,512]{2,1,0:T(8,128)(2,1)}, bf16[4,2,32,128]{3,2,1,0:T(8,128)(2,1)}, bf16[4,8,2,16,128]{4,3,2,1,0:T(8,128)(2,1)}) custom-call(bf16[1,1024,1024]{2,1,0:T(8,128)(2,1)} %li.1, bf16[1,1024,512]{2,1,0:T(8,128)(2,1)} %rhs.1, bf16[1,1024,1024]{2,1,0:T(8,128)(2,1)} %tiles.1, bf16[2,32,1024]{2,1,0:T(8,128)(2,1)} %bitcast.2, ...), custom_call_target="tpu_custom_call" | custom-call | flops 2700000000 | bytes 8000000 | tf_op jit(solution)/shard_map/forward_substitution/pallas_call | solution.py:392
  65.8 2.3 %results.1 = (bf16[1,1024,512]{2,1,0:T(8,128)(2,1)}, bf16[2,32,512]{2,1,0:T(8,128)(2,1)}, bf16[2,128,512]{2,1,0:T(8,128)(2,1)}) custom-call(bf16[1,1024,512]{2,1,0:T(8,128)(2,1)} %get-tuple-element.6.leaf, bf16[4,2,32,128]{3,2,1,0:T(8,128)(2,1)} %get-tuple-element.7.mid, bf16[4,8,2,16,128]{4,3,2,1,0:T(8,128)(2,1)} %get-tuple-element.8.top), custom_call_target="tpu_custom_call" | custom-call | tf_op jit(solution)/shard_map/results/pallas_call | solution.py:447

commit v5 on v4

--- a/solution.py
+++ b/solution.py
@@ -58,7 +58,7 @@
     barrier = pltpu.get_barrier_semaphore()
     for other in y_peers:
         pl.semaphore_signal(barrier, inc=1, device_id=at_y(other), device_id_type=MESH)
-    for d in range(1, NZ):
+    for d in (1, NZ - 1):
         pl.semaphore_signal(barrier, inc=1, device_id=at_z((z + d) % NZ), device_id_type=MESH)
     for d in range(1, NC):
         pl.semaphore_signal(barrier, inc=1, device_id=at_c((col + d) % NC), device_id_type=MESH)
@@ -97,10 +97,7 @@
     leaf_copy = pltpu.make_async_copy(xv, leaf_o.at[0], own_sem.at[0])
     leaf_copy.start()
 
-    pl.semaphore_wait(barrier, NY + NZ + NC - 3)
-
-    for d in range(1, NX):
-        pl.semaphore_signal(ring_in, inc=1, device_id=at_c((x + d) % NX * NK + k), device_id_type=MESH)
+    pl.semaphore_wait(barrier, NY + 2 + NC - 2)
 
     sends = []
 
@@ -210,6 +207,9 @@
     for b in range(2):
         total = both[b] + rup[NZ // 2 - 1, b].astype(F32) + rdown[NZ // 2 - 1, b].astype(F32)
         rbuf[b, mine, :] = (mrv[b].astype(F32) - total).astype(BF16)
+    for d in range(1, NX):
+        pl.semaphore_signal(ring_in, inc=1, device_id=at_c((x + d) % NX * NK + k), device_id_type=MESH)
+
     for step in (2, 1, 7, 6, 5):
 
         @pl.when(z + step < NZ)

time: 68.2 us -> 68.1 us (level)
  no operation moved by 1% of the time
where the time goes in v5:
time: 68.1 us; the launch traced here: 68 us
  Pallas kernels  66.7 us (98%)
  between operations  1.29 us (2%)
    pallas_call x1, Pallas kernels, local(): pl.pallas_call(kernel, out_shape=(jax.ShapeDtypeStruct((1, W, SRC), BF16)...  64.4 us
    pallas_call x1, Pallas kernels, local(): pl.pallas_call(hand_over, out_shape=(jax.ShapeDtypeStruct((1, W, SRC), BF...  2.31 us

profile of v5, /device:TPU:1, one launch (start us, length us, event | category | flops | bytes accessed | tf_op | source)
XLA Modules:
  0.0 68.0 jit_solution(9345442899777012364)
XLA Ops:
  1.3 64.4 %forward_substitution.1 = (bf16[1,1024,512]{2,1,0:T(8,128)(2,1)}, bf16[4,2,32,128]{3,2,1,0:T(8,128)(2,1)}, bf16[4,8,2,16,128]{4,3,2,1,0:T(8,128)(2,1)}) custom-call(bf16[1,1024,1024]{2,1,0:T(8,128)(2,1)} %li.1, bf16[1,1024,512]{2,1,0:T(8,128)(2,1)} %rhs.1, bf16[1,1024,1024]{2,1,0:T(8,128)(2,1)} %tiles.1, bf16[2,32,1024]{2,1,0:T(8,128)(2,1)} %bitcast.2, ...), custom_call_target="tpu_custom_call" | custom-call | flops 2700000000 | bytes 8000000 | tf_op jit(solution)/shard_map/forward_substitution/pallas_call | solution.py:392
  65.6 2.3 %results.1 = (bf16[1,1024,512]{2,1,0:T(8,128)(2,1)}, bf16[2,32,512]{2,1,0:T(8,128)(2,1)}, bf16[2,128,512]{2,1,0:T(8,128)(2,1)}) custom-call(bf16[1,1024,512]{2,1,0:T(8,128)(2,1)} %get-tuple-element.6.leaf, bf16[4,2,32,128]{3,2,1,0:T(8,128)(2,1)} %get-tuple-element.7.mid, bf16[4,8,2,16,128]{4,3,2,1,0:T(8,128)(2,1)} %get-tuple-element.8.top), custom_call_target="tpu_custom_call" | custom-call | tf_op jit(solution)/shard_map/results/pallas_call | solution.py:447
